TPU v7x, 512 devices: a whole 4x4x16 slice. The times are simulated.
512 devices in a mesh: tok: 2 (over core), head: 16 (over y, x), exp: 16 (over z).
Axes of the slice: x: 4, y: 4, z: 16, core: 2. Of those that a mesh axis runs over, the one named last changes fastest.
Arguments:
- context: bfloat16 [16, 64, 4096], P('exp', 'tok', 'head'), may hold values from -6 to 6
- out_proj: bfloat16 [4096, 4096], P('head', 'exp'), may hold values from -0.125 to 0.125
- stream: float32 [16, 64, 4096], P('exp', 'tok', 'head'), may hold values from -75 to 75
- norm_gain: float32 [4096], replicated, may hold values from 0.1 to 1.9
- expert_ids: int32 [16, 64, 8], P('exp', 'tok'), may hold values from 0 to 31, as said below
- slot_ids: int32 [16, 64, 8], P('exp', 'tok'), may hold values from -1 to 11, as said below
- gate_probs: float32 [16, 64, 8], P('exp', 'tok'), may hold values from 0.02 to 0.3
- w_gate: bfloat16 [32, 3072, 4096], P(('tok', 'exp'), 'head'), may hold values from -0.09375 to 0.09375
- w_up: bfloat16 [32, 3072, 4096], P(('tok', 'exp'), 'head'), may hold values from -0.09375 to 0.09375
- w_down: bfloat16 [32, 3072, 4096], P(('tok', 'exp'), 'head'), may hold values from -0.15625 to 0.15625
Outputs:
- mixed: float32 [16, 64, 4096], P('exp', 'tok', 'head')
Inputs may be any that keep to these rules, and one draw needn't show every extreme that they name: `expert_ids`: each token names 8 different experts. `slot_ids`: within a block of 32 consecutive tokens of one image, the choices of one expert take slots 0, 1, 2, ... in token order until its 12 slots are full, later ones get -1; in every block some expert fills all 12 slots.
All inputs are finite; a program needn't handle non-finite values.
Results may differ from a plain program's by a relative error of at most 0.0034.
Values may be sent and summed in bfloat16 or wider, within the bound.
No kernel may reach another device: no remote copies, remote signals or barrier semaphores. Data moves between devices by JAX's collectives and lax.ppermute only.
A program may use at most 64 MiB of HBM per device.

v0:
```python
import jax
import jax.numpy as jnp
from jax import lax
from jax.sharding import Mesh
from jax.sharding import PartitionSpec as P

EXPERTS = 32
TOP = 8
CAP = 12
HEAD = ("head_0", "head_1")
eps_value = 1e-05


def cut_along(x, dim, count):
    shape = x.shape
    pieces = x.reshape(*shape[:dim], count, shape[dim] // count, *shape[dim + 1 :])
    return jnp.moveaxis(pieces, dim, 0)


def sum_at_owner(x, axis, dim):
    pieces = cut_along(x, dim, lax.axis_size(axis))
    arrived = lax.all_to_all(pieces, axis, split_axis=0, concat_axis=0, tiled=True)
    return arrived.astype(jnp.float32).sum(axis=0)


def over_axes(x, axes):
    for axis in axes:
        x = lax.psum(x, axis)
    return x


def gather_axes(x, axes, dim):
    result = x
    for number in range(len(axes) - 1, -1, -1):
        result = lax.all_gather(result, axes[number], axis=dim, tiled=True)
    return result


def on_device(
    context, out_proj, stream, norm_gain, expert_ids, slot_ids, gate_probs, w_gate, w_up, w_down
):
    local_context = context[0]
    own_stream = stream[0]
    col_width = own_stream.shape[1]
    full_width = col_width * lax.axis_size(HEAD)
    col_start = lax.axis_index(HEAD) * col_width
    partial_value = jnp.dot(
        local_context,
        lax.all_gather(out_proj, "exp", axis=1, tiled=True),
        preferred_element_type=jnp.float32,
    )
    resid_own = sum_at_owner(partial_value.astype(jnp.bfloat16), HEAD, 1) + own_stream
    total_sq = over_axes(jnp.sum(resid_own * resid_own, axis=1, keepdims=True), HEAD)
    gain_own = lax.dynamic_slice_in_dim(norm_gain, col_start, col_width, 0)
    normed_own = (resid_own * lax.rsqrt(total_sq / full_width + eps_value) * gain_own).astype(
        jnp.bfloat16
    )
    choice_ids = expert_ids[0]
    choice_slots = slot_ids[0]
    weights = gate_probs[0]
    spill_slot = EXPERTS * CAP
    target = jnp.where(choice_slots >= 0, choice_ids * CAP + choice_slots, spill_slot)
    outgoing = (
        jnp.zeros((spill_slot + 1, col_width), jnp.bfloat16)
        .at[target.reshape(-1)]
        .set(jnp.repeat(normed_own, TOP, axis=0))
    )
    outgoing = outgoing[:spill_slot].reshape(EXPERTS, CAP, col_width)
    tok_count = lax.axis_size("tok")
    groups = tok_count * lax.axis_size("exp")
    local_experts = w_gate.shape[0]
    arrived = lax.all_to_all(outgoing, ("tok", "exp"), split_axis=0, concat_axis=0, tiled=True)
    arrived = arrived.reshape(groups, local_experts, CAP, col_width)
    piece = gather_axes(arrived, HEAD, 3)
    gate_more = jnp.einsum("slcd,lhd->slch", piece, w_gate, preferred_element_type=jnp.float32)
    up_more = jnp.einsum("slcd,lhd->slch", piece, w_up, preferred_element_type=jnp.float32)
    hidden = (jax.nn.silu(gate_more) * up_more).astype(jnp.bfloat16)
    produced = jnp.einsum(
        "slch,lhd->slcd", hidden, w_down, preferred_element_type=jnp.float32
    ).astype(jnp.bfloat16)
    widened = lax.optimization_barrier(produced).astype(jnp.float32)
    summed = sum_at_owner(widened.astype(jnp.bfloat16), HEAD, 3)
    returned_share = lax.all_to_all(
        summed.reshape(EXPERTS, CAP, col_width).astype(jnp.bfloat16),
        ("tok", "exp"),
        split_axis=0,
        concat_axis=0,
        tiled=True,
    ).astype(jnp.float32)
    lookup_share = jnp.concatenate(
        [returned_share.reshape(spill_slot, col_width), jnp.zeros((1, col_width), jnp.float32)],
        axis=0,
    )
    picked_share = lookup_share[target]
    expert_own = jnp.sum(picked_share * weights[:, :, None], axis=1)
    return (resid_own + expert_own)[None]


def solution(mesh):
    split = Mesh(
        mesh.devices.reshape(mesh.shape["tok"], 4, 4, mesh.shape["exp"]),
        ("tok", "head_0", "head_1", "exp"),
    )
    in_specs = (
        P("exp", "tok", HEAD),
        P(HEAD, "exp"),
        P("exp", "tok", HEAD),
        P(),
        P("exp", "tok", None),
        P("exp", "tok", None),
        P("exp", "tok", None),
        P(("tok", "exp"), HEAD, None),
        P(("tok", "exp"), HEAD, None),
        P(("tok", "exp"), HEAD, None),
    )
    out_specs = P("exp", "tok", HEAD)
    return jax.shard_map(
        on_device, mesh=split, in_specs=in_specs, out_specs=out_specs, check_vma=False
    )
```

profile of v0, /device:TPU:1, one launch (start us, length us, event | category | flops | bytes accessed | tf_op | source)
XLA Modules:
  0.0 316.5 jit_solution(14243525346558986769)
XLA Ops:
  6.5 0.0 copy-start
  6.5 0.0 copy-start.4
  6.5 0.0 copy-start.3
  6.5 0.0 copy-start.1
  6.5 0.0 all-gather.5.cloned.1.call-start
  6.6 0.7 all-gather.5.cloned.1.call-update
  7.3 76.2 %all-gather.5.cloned.1.call-done = bf16[256,4096]{1,0:T(8,128)(2,1)} async-done(((bf16[256,256]{1,0:T(8,128)(2,1)}), bf16[256,4096]{1,0:T(8,128)(2,1)}) %all-gather.5.cloned.1.call-update) | async-done | bytes 2097168 | tf_op jit(solution)/shard_map/all_gather | solution.py:49
  83.5 2.1 convolution_convert_fusion.1
  85.6 0.7 copy.38
  86.3 6.5 %all-to-all-start = ((bf16[16,32,256]{2,1,0:T(8,128)(2,1)}), bf16[16,32,256]{2,1,0:T(8,128)(2,1)S(1)}, u32[]{:S(2)}, u32[]{:S(2)}) async-start(bf16[16,32,256]{2,1,0:T(8,128)(2,1)} %bitcast.101), calls=%async_computation | async-start | bytes 524288 | tf_op jit(solution)/shard_map/all_to_all | solution.py:22
  92.8 0.0 all-gather.7.cloned.1.call-start
  92.9 0.0 copy-done.4
  92.9 0.0 copy-done.3
  92.9 0.1 copy.25
  93.0 0.1 select_n.49
  93.1 0.8 dynamic_slice.3
  93.9 6.5 %all-to-all-done = bf16[16,32,256]{2,1,0:T(8,128)(2,1)S(1)} async-done(((bf16[16,32,256]{2,1,0:T(8,128)(2,1)}), bf16[16,32,256]{2,1,0:T(8,128)(2,1)S(1)}, u32[]{:S(2)}, u32[]{:S(2)}) %all-to-all-start) | async-done | bytes 262176 | tf_op jit(solution)/shard_map/all_to_all | solution.py:22
  100.4 0.0 copy-done.1
  100.4 0.1 multiply_reduce_fusion
  100.5 6.6 %psum.14 = f32[32,1]{0,1:T(1,128)S(1)} all-reduce(f32[32,1]{0,1:T(1,128)S(1)} %bitcast.107), channel_id=1, replica_groups=mesh['tok'=2,'head_0'=4,'head_1'=4,'exp'=16] {'head_0'}, use_global_device_ids=true, to_apply=%region_2.0 | all-reduce | flops 32 | bytes 256 | tf_op jit(solution)/shard_map/psum | solution.py:28
  107.1 7.0 %psum.15 = f32[32,1]{0,1:T(1,128)S(1)} all-reduce(f32[32,1]{0,1:T(1,128)S(1)} %psum.14), channel_id=1, replica_groups=mesh['tok'=2,'head_0'=4,'head_1'=4,'exp'=16] {'head_1'}, use_global_device_ids=true, to_apply=%region_3.0 | all-reduce | flops 32 | bytes 256 | tf_op jit(solution)/shard_map/psum | solution.py:28
  114.1 0.1 multiply_convert_fusion
  114.2 1.5 scatter_custom_fusion
  115.8 0.0 copy-start.5
  115.8 44.8 %all_to_all.20 = bf16[32,12,256]{2,1,0:T(8,128)(2,1)S(1)} all-to-all(bf16[32,12,256]{2,1,0:T(8,128)(2,1)S(1)} %reshape.147), channel_id=1, replica_groups=mesh['tok'=2,'head_0'=4,'head_1'=4,'exp'=16] {'tok','exp'}, dimensions={0} | all-to-all | bytes 393216 | tf_op jit(solution)/shard_map/all_to_all | solution.py:72
  160.6 0.1 copy.26
  160.6 13.4 %all-gather = bf16[32,12,1024]{2,0,1:T(8,128)(2,1)} all-gather(bf16[32,12,256]{2,0,1:T(8,128)(2,1)S(1)} %copy.26), channel_id=2, replica_groups=mesh['tok'=2,'head_0'=4,'head_1'=4,'exp'=16] {'head_1'}, dimensions={2}, use_global_device_ids=true | all-gather | bytes 983040 | tf_op jit(solution)/shard_map/all_gather | solution.py:35
  174.0 0.0 all-gather.7.cloned.1.call-update
  174.0 36.9 %all-gather.7.cloned.1.call-done = bf16[32,12,4096]{2,0,1:T(8,128)(2,1)} async-done(((bf16[32,12,1024]{2,0,1:T(8,128)(2,1)}), bf16[32,12,4096]{2,0,1:T(8,128)(2,1)}) %all-gather.7.cloned.1.call-update) | async-done | bytes 3145744 | tf_op jit(solution)/shard_map/all_gather | solution.py:35
  210.9 0.0 copy-done.5
  210.9 3.7 %fusion.6 = f32[32,1,12,192]{3,0,2,1:T(8,128)} fusion(bf16[32,12,4096]{2,0,1:T(8,128)(2,1)} %all-gather.7.cloned.1.call-done, bf16[1,192,4096]{2,1,0:T(8,128)(2,1)S(1)} %copy-done.5), kind=kOutput, calls=%fused_computation.11 | convolution fusion | flops 603979776 | bytes 5013504 | tf_op jit(solution)/shard_map/slcd,lhd->slch/dot_general | solution.py:75
  214.6 0.0 copy-done
  214.6 7.6 %fusion = bf16[32,1,12,4096]{3,0,2,1:T(8,128)(2,1)} fusion(bf16[1,192,4096]{2,1,0:T(8,128)(2,1)S(1)} %copy-done, bf16[32,12,4096]{2,0,1:T(8,128)(2,1)} %all-gather.7.cloned.1.call-done, bf16[1,192,4096]{2,1,0:T(8,128)(2,1)} %param.18, f32[32,1,12,192]{3,0,2,1:T(8,128)} %fusion.6), kind=kOutput, calls=%fused_computation.3 | convolution fusion | flops 1209974784 | bytes 9732096 | tf_op jit(solution)/shard_map/slch,lhd->slcd/dot_general | solution.py:78
  222.2 2.3 copy.37
  224.5 44.0 %all_to_all.21 = bf16[16,32,1,12,256]{4,1,3,2,0:T(8,128)(2,1)} all-to-all(bf16[16,32,1,12,256]{4,1,3,2,0:T(8,128)(2,1)S(1)} %bitcast.102), channel_id=1, replica_groups=mesh['tok'=2,'head_0'=4,'head_1'=4,'exp'=16] {'head_0','head_1'}, dimensions={0} | all-to-all | bytes 6291456 | tf_op jit(solution)/shard_map/all_to_all | solution.py:22
  268.5 0.0 copy-start.2
  268.5 2.6 reduce_sum.46
  271.0 0.8 copy.29
  271.8 14.3 %all-to-all-start.3 = ((bf16[32,12,256]{2,1,0:T(8,128)(2,1)}), bf16[32,12,256]{2,1,0:T(8,128)(2,1)S(1)}, u32[]{:S(2)}, u32[]{:S(2)}) async-start(bf16[32,12,256]{2,1,0:T(8,128)(2,1)} %copy.29), calls=%async_computation.3 | async-start | bytes 524288 | tf_op jit(solution)/shard_map/all_to_all | solution.py:83
  286.2 0.1 copy.30
  286.2 0.1 reshape.158
  286.3 0.0 copy-done.2
  286.3 0.1 copy.31
  286.4 21.4 %all-to-all-done.3 = bf16[32,12,256]{2,1,0:T(8,128)(2,1)S(1)} async-done(((bf16[32,12,256]{2,1,0:T(8,128)(2,1)}), bf16[32,12,256]{2,1,0:T(8,128)(2,1)S(1)}, u32[]{:S(2)}, u32[]{:S(2)}) %all-to-all-start.3) | async-done | bytes 196640 | tf_op jit(solution)/shard_map/all_to_all | solution.py:83
  307.9 1.0 gather_fusion
  308.9 0.1 fusion.28
  309.0 0.6 bitcast_add_fusion
  (9 shorter events, 0.2 us)
Async XLA Ops:
  6.5 208.1 %copy-start = (bf16[1,192,4096]{2,1,0:T(8,128)(2,1)S(1)}, bf16[1,192,4096]{2,1,0:T(8,128)(2,1)}, u32[]{:S(2)}) copy-start(bf16[1,192,4096]{2,1,0:T(8,128)(2,1)} %param.19) | copy-start | bytes 4718596
  6.5 86.4 %copy-start.4 = (s32[1,32,8]{1,2,0:T(8,128)S(1)}, s32[1,32,8]{1,2,0:T(8,128)}, u32[]{:S(2)}) copy-start(s32[1,32,8]{1,2,0:T(8,128)} %param.14) | copy-start | bytes 3076
  6.5 86.4 %copy-start.3 = (s32[1,32,8]{1,2,0:T(8,128)S(1)}, s32[1,32,8]{1,2,0:T(8,128)}, u32[]{:S(2)}) copy-start(s32[1,32,8]{1,2,0:T(8,128)} %param.15) | copy-start | bytes 3076
  6.5 93.9 %copy-start.1 = (f32[1,32,256]{2,1,0:T(8,128)S(1)}, f32[1,32,256]{2,1,0:T(8,128)}, u32[]{:S(2)}) copy-start(f32[1,32,256]{2,1,0:T(8,128)} %param.12) | copy-start | bytes 98308
  6.5 77.0 %all-gather.5.cloned.1.call-start = ((), (), s32[]{:S(2)}) async-start(), calls=%async_computation.4 | async-start | bytes 2228224 | tf_op jit(solution)/shard_map/all_gather | solution.py:49
  86.3 14.1 %all-to-all-start = ((bf16[16,32,256]{2,1,0:T(8,128)(2,1)}), bf16[16,32,256]{2,1,0:T(8,128)(2,1)S(1)}, u32[]{:S(2)}, u32[]{:S(2)}) async-start(bf16[16,32,256]{2,1,0:T(8,128)(2,1)} %bitcast.101), calls=%async_computation | async-start | bytes 524288 | tf_op jit(solution)/shard_map/all_to_all | solution.py:22
  92.8 118.1 %all-gather.7.cloned.1.call-start = ((), (), s32[]{:S(2)}) async-start(), calls=%async_computation.5 | async-start | bytes 3932160 | tf_op jit(solution)/shard_map/all_gather | solution.py:35
  115.8 95.2 %copy-start.5 = (bf16[1,192,4096]{2,1,0:T(8,128)(2,1)S(1)}, bf16[1,192,4096]{2,1,0:T(8,128)(2,1)}, u32[]{:S(2)}) copy-start(bf16[1,192,4096]{2,1,0:T(8,128)(2,1)} %param.17) | copy-start | bytes 4718596
  268.5 17.9 %copy-start.2 = (f32[1,32,8]{1,2,0:T(8,128)S(1)}, f32[1,32,8]{1,2,0:T(8,128)}, u32[]{:S(2)}) copy-start(f32[1,32,8]{1,2,0:T(8,128)} %param.16) | copy-start | bytes 3076
  271.8 36.0 %all-to-all-start.3 = ((bf16[32,12,256]{2,1,0:T(8,128)(2,1)}), bf16[32,12,256]{2,1,0:T(8,128)(2,1)S(1)}, u32[]{:S(2)}, u32[]{:S(2)}) async-start(bf16[32,12,256]{2,1,0:T(8,128)(2,1)} %copy.29), calls=%async_computation.3 | async-start | bytes 524288 | tf_op jit(solution)/shard_map/all_to_all | solution.py:83
Sparse Core Ops, SparseCore 0:
  9.4 74.0 all-gather.4
  174.2 36.7 all-gather.6
where the time goes:
time: 317 us; the launch traced here: 316 us
  waiting for transfers between devices  142 us (45%)
  blocking collectives  116 us (37%)
  starting transfers between devices  20.9 us (7%)
  between operations  13.6 us (4%)
  matrix products  13.3 us (4%)
  local copies, waits for them, and re-layouts  7.68 us (2%)
  other arithmetic  3.61 us (1%)
    all_gather x1, waiting for transfers between devices, on_device(): lax.all_gather(out_proj, 'exp', axis=1, tiled=True)  76.2 us
    all_to_all x1, blocking collectives, on_device(): lax.all_to_all(outgoing, ('tok', 'exp'), split_axis=0, concat_axis=0, til...  44.8 us
    all_to_all x1, blocking collectives, sum_at_owner(): lax.all_to_all(pieces, axis, split_axis=0, concat_axis=0, tiled=True)  44 us
    all_gather x1, waiting for transfers between devices, gather_axes(): result = lax.all_gather(result, axes[number], axis=dim, tiled=True)  36.9 us
    all_to_all x1, waiting for transfers between devices, on_device(): lax.all_to_all(summed.reshape(EXPERTS, CAP, col_width).astype(jnp.bfloat1...  21.4 us
    all_to_all x1, starting transfers between devices, on_device(): lax.all_to_all(summed.reshape(EXPERTS, CAP, col_width).astype(jnp.bfloat1...  14.3 us
    psum x2, blocking collectives, over_axes(): x = lax.psum(x, axis)  13.5 us
    all_gather x1, blocking collectives, gather_axes(): result = lax.all_gather(result, axes[number], axis=dim, tiled=True)  13.4 us
  transfers between devices with their start and end apart: 4, of which 4 were waited for; matrix products, arithmetic and copies ran while one was open for 0% of the time, Pallas kernels for 0%

commit v1 on v0

--- a/solution.py
+++ b/solution.py
@@ -46,7 +46,10 @@
     col_start = lax.axis_index(HEAD) * col_width
     partial_value = jnp.dot(
         local_context,
-        lax.all_gather(out_proj, "exp", axis=1, tiled=True),
+        jnp.concatenate(
+            lax.all_to_all(jnp.stack([out_proj for _ in range(lax.axis_size("exp"))]), "exp", 0, 0),
+            axis=1,
+        ),
         preferred_element_type=jnp.float32,
     )
     resid_own = sum_at_owner(partial_value.astype(jnp.bfloat16), HEAD, 1) + own_stream

time: 317 us -> 342 us (1.079)
  blocking collectives: 116 us -> 217 us
  waiting for transfers between devices: 142 us -> 64.8 us
    all_to_all x0 -> x1, blocking collectives: none -> 106 us  [on_device(): lax.all_to_all(jnp.stack([out_proj for _ in range(lax.axis_size('exp'))])...]
    all_gather x1 -> x0, waiting for transfers between devices: 76.2 us -> none  [on_device(): lax.all_gather(out_proj, 'exp', axis=1, tiled=True)]
    all_to_all x1, blocking collectives: 44.8 us -> 39.8 us  [on_device(): lax.all_to_all(outgoing, ('tok', 'exp'), split_axis=0, concat_axis=0, til...]
  transfers between devices with their start and end apart: 4 -> 3, of which waited for: 4 -> 3; matrix products, arithmetic and copies ran while one was open for 0% -> 0% of each run, Pallas kernels for 0% -> 0%
where the time goes in v1:
time: 342 us; the launch traced here: 341 us
  blocking collectives  217 us (63%)
  waiting for transfers between devices  64.8 us (19%)
  starting transfers between devices  21.1 us (6%)
  between operations  13.6 us (4%)
  matrix products  11.9 us (3%)
  local copies, waits for them, and re-layouts  9.01 us (3%)
  other arithmetic  3.61 us (1%)
    all_to_all x1, blocking collectives, on_device(): lax.all_to_all(jnp.stack([out_proj for _ in range(lax.axis_size('exp'))])...  106 us
    all_to_all x1, blocking collectives, sum_at_owner(): lax.all_to_all(pieces, axis, split_axis=0, concat_axis=0, tiled=True)  44 us
    all_to_all x1, blocking collectives, on_device(): lax.all_to_all(outgoing, ('tok', 'exp'), split_axis=0, concat_axis=0, til...  39.8 us
    all_gather x1, waiting for transfers between devices, gather_axes(): result = lax.all_gather(result, axes[number], axis=dim, tiled=True)  36.9 us
    all_to_all x1, waiting for transfers between devices, on_device(): lax.all_to_all(summed.reshape(EXPERTS, CAP, col_width).astype(jnp.bfloat1...  21.4 us
    all_to_all x1, starting transfers between devices, on_device(): lax.all_to_all(summed.reshape(EXPERTS, CAP, col_width).astype(jnp.bfloat1...  14.3 us
    psum x2, blocking collectives, over_axes(): x = lax.psum(x, axis)  14 us
    all_gather x1, blocking collectives, gather_axes(): result = lax.all_gather(result, axes[number], axis=dim, tiled=True)  13.4 us
  transfers between devices with their start and end apart: 3, of which 3 were waited for; matrix products, arithmetic and copies ran while one was open for 0% of the time, Pallas kernels for 0%

profile of v1, /device:TPU:1, one launch (start us, length us, event | category | flops | bytes accessed | tf_op | source)
XLA Modules:
  0.0 341.1 jit_solution(10242948599187341488)
XLA Ops:
  6.5 0.0 copy-start
  6.5 1.1 copy.26
  7.7 0.2 stack.2
  7.9 0.0 copy-start.2
  7.9 105.8 %all_to_all.25 = bf16[16,256,256]{1,2,0:T(8,128)(2,1)S(1)} all-to-all(bf16[16,256,256]{1,2,0:T(8,128)(2,1)S(1)} %stack.2), channel_id=1, replica_groups=mesh['tok'=2,'head_0'=4,'head_1'=4,'exp'=16] {'exp'}, dimensions={0} | all-to-all | bytes 4194304 | tf_op jit(solution)/shard_map/all_to_all | solution.py:50
  113.7 0.0 copy-start.4
  113.7 0.0 copy-start.5
  113.7 0.0 copy-start.1
  113.7 0.0 copy-done.2
  113.7 0.7 convolution_convert_fusion.1
  114.4 0.7 copy.41
  115.1 6.8 %all-to-all-start.1 = ((bf16[16,32,256]{2,1,0:T(8,128)(2,1)}), bf16[16,32,256]{2,1,0:T(8,128)(2,1)S(1)}, u32[]{:S(2)}, u32[]{:S(2)}) async-start(bf16[16,32,256]{2,1,0:T(8,128)(2,1)} %bitcast.104), calls=%async_computation.1 | async-start | bytes 524288 | tf_op jit(solution)/shard_map/all_to_all | solution.py:22
  121.9 0.0 all-gather.4.cloned.1.call-start
  121.9 0.0 copy-done.4
  122.0 0.0 copy-done.5
  122.0 0.1 copy.28
  122.1 0.1 select_n.49
  122.2 0.8 dynamic_slice.3
  122.9 6.5 %all-to-all-done.1 = bf16[16,32,256]{2,1,0:T(8,128)(2,1)S(1)} async-done(((bf16[16,32,256]{2,1,0:T(8,128)(2,1)}), bf16[16,32,256]{2,1,0:T(8,128)(2,1)S(1)}, u32[]{:S(2)}, u32[]{:S(2)}) %all-to-all-start.1) | async-done | bytes 262176 | tf_op jit(solution)/shard_map/all_to_all | solution.py:22
  129.5 0.0 copy-done.1
  129.5 0.1 multiply_reduce_fusion
  129.6 7.3 %psum.14 = f32[32,1]{0,1:T(1,128)S(1)} all-reduce(f32[32,1]{0,1:T(1,128)S(1)} %bitcast.111), channel_id=1, replica_groups=mesh['tok'=2,'head_0'=4,'head_1'=4,'exp'=16] {'head_0'}, use_global_device_ids=true, to_apply=%region_2.0 | all-reduce | flops 32 | bytes 256 | tf_op jit(solution)/shard_map/psum | solution.py:28
  136.9 6.7 %psum.15 = f32[32,1]{0,1:T(1,128)S(1)} all-reduce(f32[32,1]{0,1:T(1,128)S(1)} %psum.14), channel_id=1, replica_groups=mesh['tok'=2,'head_0'=4,'head_1'=4,'exp'=16] {'head_1'}, use_global_device_ids=true, to_apply=%region_3.0 | all-reduce | flops 32 | bytes 256 | tf_op jit(solution)/shard_map/psum | solution.py:28
  143.7 0.1 multiply_convert_fusion
  143.7 1.5 scatter_custom_fusion
  145.3 0.0 copy-start.6
  145.3 39.8 %all_to_all.26 = bf16[32,12,256]{2,1,0:T(8,128)(2,1)S(1)} all-to-all(bf16[32,12,256]{2,1,0:T(8,128)(2,1)S(1)} %reshape.157), channel_id=1, replica_groups=mesh['tok'=2,'head_0'=4,'head_1'=4,'exp'=16] {'tok','exp'}, dimensions={0} | all-to-all | bytes 393216 | tf_op jit(solution)/shard_map/all_to_all | solution.py:75
  185.2 0.1 copy.29
  185.2 13.4 %all-gather = bf16[32,12,1024]{2,0,1:T(8,128)(2,1)} all-gather(bf16[32,12,256]{2,0,1:T(8,128)(2,1)S(1)} %copy.29), channel_id=2, replica_groups=mesh['tok'=2,'head_0'=4,'head_1'=4,'exp'=16] {'head_1'}, dimensions={2}, use_global_device_ids=true | all-gather | bytes 983040 | tf_op jit(solution)/shard_map/all_gather | solution.py:35
  198.6 0.0 all-gather.4.cloned.1.call-update
  198.6 36.9 %all-gather.4.cloned.1.call-done = bf16[32,12,4096]{2,0,1:T(8,128)(2,1)} async-done(((bf16[32,12,1024]{2,0,1:T(8,128)(2,1)}), bf16[32,12,4096]{2,0,1:T(8,128)(2,1)}) %all-gather.4.cloned.1.call-update) | async-done | bytes 3145744 | tf_op jit(solution)/shard_map/all_gather | solution.py:35
  235.5 0.0 copy-done.6
  235.6 3.7 %fusion.6 = f32[32,1,12,192]{3,0,2,1:T(8,128)} fusion(bf16[32,12,4096]{2,0,1:T(8,128)(2,1)} %all-gather.4.cloned.1.call-done, bf16[1,192,4096]{2,1,0:T(8,128)(2,1)S(1)} %copy-done.6), kind=kOutput, calls=%fused_computation.11 | convolution fusion | flops 603979776 | bytes 5013504 | tf_op jit(solution)/shard_map/slcd,lhd->slch/dot_general | solution.py:78
  239.2 0.0 copy-done
  239.2 7.6 %fusion = bf16[32,1,12,4096]{3,0,2,1:T(8,128)(2,1)} fusion(bf16[1,192,4096]{2,1,0:T(8,128)(2,1)S(1)} %copy-done, bf16[32,12,4096]{2,0,1:T(8,128)(2,1)} %all-gather.4.cloned.1.call-done, bf16[1,192,4096]{2,1,0:T(8,128)(2,1)} %param.18, f32[32,1,12,192]{3,0,2,1:T(8,128)} %fusion.6), kind=kOutput, calls=%fused_computation.3 | convolution fusion | flops 1209974784 | bytes 9732096 | tf_op jit(solution)/shard_map/slch,lhd->slcd/dot_general | solution.py:81
  246.8 2.3 copy.40
  249.1 44.0 %all_to_all.27 = bf16[16,32,1,12,256]{4,1,3,2,0:T(8,128)(2,1)} all-to-all(bf16[16,32,1,12,256]{4,1,3,2,0:T(8,128)(2,1)S(1)} %bitcast.105), channel_id=1, replica_groups=mesh['tok'=2,'head_0'=4,'head_1'=4,'exp'=16] {'head_0','head_1'}, dimensions={0} | all-to-all | bytes 6291456 | tf_op jit(solution)/shard_map/all_to_all | solution.py:22
  293.1 2.6 reduce_sum.46
  295.6 0.8 copy.32
  296.4 14.3 %all-to-all-start.4 = ((bf16[32,12,256]{2,1,0:T(8,128)(2,1)}), bf16[32,12,256]{2,1,0:T(8,128)(2,1)S(1)}, u32[]{:S(2)}, u32[]{:S(2)}) async-start(bf16[32,12,256]{2,1,0:T(8,128)(2,1)} %copy.32), calls=%async_computation.4 | async-start | bytes 524288 | tf_op jit(solution)/shard_map/all_to_all | solution.py:86
  310.8 0.1 copy.33
  310.9 0.1 reshape.168
  310.9 0.0 copy-done.3
  311.0 0.1 copy.34
  311.0 21.4 %all-to-all-done.4 = bf16[32,12,256]{2,1,0:T(8,128)(2,1)S(1)} async-done(((bf16[32,12,256]{2,1,0:T(8,128)(2,1)}), bf16[32,12,256]{2,1,0:T(8,128)(2,1)S(1)}, u32[]{:S(2)}, u32[]{:S(2)}) %all-to-all-start.4) | async-done | bytes 196640 | tf_op jit(solution)/shard_map/all_to_all | solution.py:86
  332.5 1.0 gather_fusion
  333.5 0.1 fusion.28
  333.7 0.6 bitcast_add_fusion
  (10 shorter events, 0.2 us)
Async XLA Ops:
  6.5 232.7 %copy-start = (bf16[1,192,4096]{2,1,0:T(8,128)(2,1)S(1)}, bf16[1,192,4096]{2,1,0:T(8,128)(2,1)}, u32[]{:S(2)}) copy-start(bf16[1,192,4096]{2,1,0:T(8,128)(2,1)} %param.19) | copy-start | bytes 4718596
  7.9 105.8 %copy-start.2 = (bf16[1,32,256]{2,1,0:T(8,128)(2,1)S(1)}, bf16[1,32,256]{2,1,0:T(8,128)(2,1)}, u32[]{:S(2)}) copy-start(bf16[1,32,256]{2,1,0:T(8,128)(2,1)} %param.10) | copy-start | bytes 49156
  113.7 8.3 %copy-start.4 = (s32[1,32,8]{1,2,0:T(8,128)S(1)}, s32[1,32,8]{1,2,0:T(8,128)}, u32[]{:S(2)}) copy-start(s32[1,32,8]{1,2,0:T(8,128)} %param.15) | copy-start | bytes 3076
  113.7 8.3 %copy-start.5 = (s32[1,32,8]{1,2,0:T(8,128)S(1)}, s32[1,32,8]{1,2,0:T(8,128)}, u32[]{:S(2)}) copy-start(s32[1,32,8]{1,2,0:T(8,128)} %param.14) | copy-start | bytes 3076
  113.7 15.8 %copy-start.1 = (f32[1,32,256]{2,1,0:T(8,128)S(1)}, f32[1,32,256]{2,1,0:T(8,128)}, u32[]{:S(2)}) copy-start(f32[1,32,256]{2,1,0:T(8,128)} %param.12) | copy-start | bytes 98308
  115.1 14.3 %all-to-all-start.1 = ((bf16[16,32,256]{2,1,0:T(8,128)(2,1)}), bf16[16,32,256]{2,1,0:T(8,128)(2,1)S(1)}, u32[]{:S(2)}, u32[]{:S(2)}) async-start(bf16[16,32,256]{2,1,0:T(8,128)(2,1)} %bitcast.104), calls=%async_computation.1 | async-start | bytes 524288 | tf_op jit(solution)/shard_map/all_to_all | solution.py:22
  121.9 113.7 %all-gather.4.cloned.1.call-start = ((), (), s32[]{:S(2)}) async-start(), calls=%async_computation.5 | async-start | bytes 3932160 | tf_op jit(solution)/shard_map/all_gather | solution.py:35
  145.3 90.2 %copy-start.6 = (bf16[1,192,4096]{2,1,0:T(8,128)(2,1)S(1)}, bf16[1,192,4096]{2,1,0:T(8,128)(2,1)}, u32[]{:S(2)}) copy-start(bf16[1,192,4096]{2,1,0:T(8,128)(2,1)} %param.17) | copy-start | bytes 4718596
  293.1 17.9 %copy-start.3 = (f32[1,32,8]{1,2,0:T(8,128)S(1)}, f32[1,32,8]{1,2,0:T(8,128)}, u32[]{:S(2)}) copy-start(f32[1,32,8]{1,2,0:T(8,128)} %param.16) | copy-start | bytes 3076
  296.4 36.0 %all-to-all-start.4 = ((bf16[32,12,256]{2,1,0:T(8,128)(2,1)}), bf16[32,12,256]{2,1,0:T(8,128)(2,1)S(1)}, u32[]{:S(2)}, u32[]{:S(2)}) async-start(bf16[32,12,256]{2,1,0:T(8,128)(2,1)} %copy.32), calls=%async_computation.4 | async-start | bytes 524288 | tf_op jit(solution)/shard_map/all_to_all | solution.py:86
Sparse Core Ops, SparseCore 0:
  198.8 36.7 all-gather.3
